TPU v7x, 32 devices: a whole 2x2x4 slice. The times are simulated.
32 devices in a mesh: temp: 4 (over y, core), dom: 8 (over z, x).
Axes of the slice: x: 2, y: 2, z: 4, core: 2. Of those that a mesh axis runs over, the one named last changes fastest.
Arguments:
- particles: bfloat16 [4, 4096, 3072], P('temp', 'dom'), may hold values from -6 to 6
- log_weights: float32 [4, 4096], P('temp', 'dom'), may hold values from -200 to 200
- offspring: int32 [4, 64], P('temp', 'dom'), may hold values from 0 to 2, as said below
- even_pairs: int32 [4, 64], P('temp', 'dom'), may hold values from 0 to 1, as said below
- odd_pairs: int32 [4, 64], P('temp', 'dom'), may hold values from 0 to 1, as said below
- inverse_temp: float32 [4], P('temp'), may hold values from 0.5 to 4
- flow_in: bfloat16 [1536, 512], replicated, may hold values from -0.15625 to 0.15625
- flow_mid: bfloat16 [512, 512], replicated, may hold values from -0.25 to 0.25
- flow_out: bfloat16 [512, 3072], replicated, may hold values from -0.25 to 0.25
- energy_in: bfloat16 [3072, 512], replicated, may hold values from -0.109375 to 0.109375
- energy_mid: bfloat16 [512, 512], replicated, may hold values from -0.25 to 0.25
- energy_out: float32 [512], replicated, may hold values from -0.25 to 0.25
Outputs:
- new_particles: bfloat16 [4, 4096, 3072], P('temp', 'dom')
- new_log_weights: float32 [4, 4096], P('temp', 'dom')
- log_ess: float32 [4], P('temp')
Inputs may be any that keep to these rules, and one draw needn't show every extreme that they name: `offspring`: counts are 0, 1 or 2 and each group's counts sum to 64. Of the 8 blocks of one device at most 1 have count 2 and at most 1 have count 0; in every group some device has exactly 1 with count 2 and some device exactly 1 with count 0. `even_pairs`: groups 2i and 2i + 1 carry equal rows. At most 2 of the 8 blocks of one device are 1, and in every pair some device has exactly 2. `odd_pairs`: groups 2i + 1 and 2i + 2 carry equal rows; groups 0 and 3 are all 0. At most 2 of the 8 blocks of one device are 1, and in every pair some device has exactly 2.
All inputs are finite; a program needn't handle non-finite values.
Results may differ from a plain program's by a relative error of at most 0.0024.
Values may be sent and summed in bfloat16 or wider, within the bound.
A program may use at most 128 MiB of HBM per device.

v0:
```python
import jax
import jax.numpy as jnp
from jax import lax
from jax.sharding import PartitionSpec as P

SURPLUS = 1
SWAPS = 2


old_level = 0.5
new_level = 0.75
scale_limit = 0.05


def with_halo(block, sides, width):
    for axis, dim in sides:
        count = lax.axis_size(axis)
        forward = [(i, i + 1) for i in range(count - 1)]
        backward = [(target, source) for source, target in forward]
        low = lax.ppermute(
            lax.slice_in_dim(block, block.shape[dim] - width, None, axis=dim), axis, forward
        )
        high = lax.ppermute(lax.slice_in_dim(block, 0, width, axis=dim), axis, backward)
        block = jnp.concatenate([low, block, high], axis=dim)
    return block


def transport(row_data, flow_in, flow_mid, flow_out):
    half_width = row_data.shape[1] // 2
    kept_half = row_data[:, :half_width]
    moved_half = row_data[:, half_width:]
    hidden_one = jax.nn.gelu(
        jnp.dot(kept_half, flow_in, preferred_element_type=jnp.float32)
    ).astype(jnp.bfloat16)
    hidden_two = jax.nn.gelu(
        jnp.dot(hidden_one, flow_mid, preferred_element_type=jnp.float32)
    ).astype(jnp.bfloat16)
    scale_shift = jnp.dot(hidden_two, flow_out, preferred_element_type=jnp.float32)
    log_scale = scale_limit * jnp.tanh(scale_shift[:, :half_width])
    offset_rows = (
        moved_half.astype(jnp.float32) * jnp.exp(log_scale) + scale_shift[:, half_width:]
    ).astype(jnp.bfloat16)
    return (jnp.concatenate([kept_half, offset_rows], axis=1), jnp.sum(log_scale, axis=1))


def energy(row_data, energy_in, energy_mid, energy_out):
    layer_one = jax.nn.gelu(
        jnp.dot(row_data, energy_in, preferred_element_type=jnp.float32)
    ).astype(jnp.bfloat16)
    layer_two = jax.nn.gelu(jnp.dot(layer_one, energy_mid, preferred_element_type=jnp.float32))
    return jnp.sum(layer_two * energy_out[None, :], axis=1)


def table_lookup(table, index):
    positions = jnp.arange(table.shape[0], dtype=jnp.int32)
    index = jnp.asarray(index)
    return jnp.sum(jnp.where(positions == index[..., None], table, 0), axis=-1)


def pick_rows(flags, rank_order, slot_count):
    slot_ids = jnp.arange(slot_count, dtype=jnp.int32)
    positions = jnp.arange(flags.shape[0], dtype=jnp.int32)
    matches = (flags[None, :] == 1) & (rank_order[None, :] == slot_ids[:, None])
    return jnp.sum(jnp.where(matches, positions[None, :], 0), axis=1)


def neighbour_swap(blocks, swap_mask, parity):
    block_rows = blocks.shape[1]
    features = blocks.shape[2]
    rank_order = jnp.cumsum(swap_mask) - 1
    chosen = pick_rows(swap_mask, rank_order, SWAPS)
    packed = jnp.take(blocks, chosen, axis=0).reshape(SWAPS * block_rows, features)
    extended = with_halo(packed, (("temp", 0),), SWAPS * block_rows)
    from_lower = extended[: SWAPS * block_rows]
    from_upper = extended[2 * SWAPS * block_rows :]
    upper_side = lax.axis_index("temp") % 2 == parity
    received = jnp.where(upper_side, from_upper, from_lower).reshape(SWAPS, block_rows, features)
    placed_at = jnp.clip(rank_order, 0, SWAPS - 1)
    return jnp.where((swap_mask == 1)[:, None, None], jnp.take(received, placed_at, axis=0), blocks)


def per_device(
    particles,
    log_weights,
    offspring,
    even_pairs,
    odd_pairs,
    inverse_temp,
    flow_in,
    flow_mid,
    flow_out,
    energy_in,
    energy_mid,
    energy_out,
):
    block_count = offspring.shape[1]
    features = particles.shape[2]
    block_rows = particles.shape[1] // block_count
    spare_rows = SURPLUS * block_rows
    blocks = particles[0].reshape(block_count, block_rows, features)
    counts = offspring[0]
    doubled = (counts == 2).astype(jnp.int32)
    discarded_rows = (counts == 0).astype(jnp.int32)
    spare_rank = jnp.cumsum(doubled) - 1
    vacant_rank = jnp.cumsum(discarded_rows) - 1
    weights = (
        log_weights[0].reshape(block_count, block_rows)
        - jnp.log(jnp.maximum(counts, 1).astype(jnp.float32))[:, None]
    )
    spare_ids = pick_rows(doubled, spare_rank, SURPLUS)
    spare_blocks = jnp.take(blocks, spare_ids, axis=0).reshape(spare_rows, features)
    spare_weights = jnp.take(weights, spare_ids, axis=0)
    own_tally = (
        jnp.stack([jnp.sum(doubled), jnp.sum(discarded_rows)]).astype(jnp.float32).reshape(1, 2)
    )
    all_tallies, all_spare_weights = (
        lax.all_gather(own_tally, "dom", axis=0, tiled=True),
        lax.all_gather(spare_weights, "dom", axis=0, tiled=True),
    )
    tally_ints = all_tallies.astype(jnp.int32)
    dom_count = lax.axis_size("dom")
    self_index = lax.axis_index("dom")
    spare_end = jnp.cumsum(tally_ints[:, 0])
    spare_start = spare_end - tally_ints[:, 0]
    vacant_start = jnp.cumsum(tally_ints[:, 1]) - tally_ints[:, 1]
    slot_ids = jnp.arange(SURPLUS, dtype=jnp.int32)
    own_rank = table_lookup(vacant_start, self_index) + slot_ids
    is_live = slot_ids < table_lookup(tally_ints[:, 1], self_index)
    device = jnp.sum((spare_end <= own_rank[..., None]).astype(jnp.int32), axis=-1)
    device = jnp.clip(device, 0, dom_count - 1)
    source_slot = own_rank - table_lookup(spare_start, device)
    wanted = device * SURPLUS + jnp.clip(source_slot, 0, SURPLUS - 1)
    wanted_rows = (
        wanted[:, None] * block_rows + jnp.arange(block_rows, dtype=jnp.int32)[None, :]
    ).reshape(spare_rows)
    flat_weights = all_spare_weights.reshape(-1)
    filled_weights = jnp.take(flat_weights, jnp.clip(wanted_rows, 0, flat_weights.shape[0] - 1))
    live_rows = jnp.repeat(is_live, block_rows)
    shard_rows = lax.all_gather(spare_blocks, "dom", axis=0, tiled=True)
    row_numbers = jnp.arange(shard_rows.shape[0], dtype=jnp.int32)
    matches = ((wanted_rows[:, None] == row_numbers[None, :]) & live_rows[:, None]).astype(
        jnp.bfloat16
    )
    filled = jnp.dot(matches, shard_rows, preferred_element_type=jnp.float32)
    fill_at = jnp.clip(vacant_rank, 0, SURPLUS - 1)
    vacant = discarded_rows == 1
    filled_blocks = filled.astype(jnp.bfloat16).reshape(SURPLUS, block_rows, features)
    blocks = jnp.where(vacant[:, None, None], jnp.take(filled_blocks, fill_at, axis=0), blocks)
    weights = jnp.where(
        vacant[:, None],
        jnp.take(filled_weights.reshape(SURPLUS, block_rows), fill_at, axis=0),
        weights,
    )
    blocks = neighbour_swap(blocks, even_pairs[0], 0)
    blocks = neighbour_swap(blocks, odd_pairs[0], 1)
    row_data = blocks.reshape(block_count * block_rows, features)
    moved, log_det = transport(row_data, flow_in, flow_mid, flow_out)
    before = energy(row_data, energy_in, energy_mid, energy_out)
    after = energy(moved, energy_in, energy_mid, energy_out)
    updated = (
        weights.reshape(-1) + log_det - inverse_temp[0] * (new_level * after - old_level * before)
    )
    peak = lax.pmax(jnp.max(updated), "dom")
    first_sum, second_sum = lax.psum(
        (jnp.sum(jnp.exp(updated - peak)), jnp.sum(jnp.exp(2.0 * (updated - peak)))), "dom"
    )
    particle_total = updated.shape[0] * dom_count
    new_log_weights = updated - (peak + jnp.log(first_sum))
    log_ess = 2.0 * jnp.log(first_sum) - jnp.log(second_sum) - jnp.log(jnp.float32(particle_total))
    return (moved.reshape(1, -1, features), new_log_weights.reshape(1, -1), log_ess.reshape(1))


def solution(mesh):
    in_specs = (
        P("temp", "dom", None),
        P("temp", "dom"),
        P("temp", "dom"),
        P("temp", "dom"),
        P("temp", "dom"),
        P("temp"),
        P(),
        P(),
        P(),
        P(),
        P(),
        P(),
    )
    out_specs = (P("temp", "dom", None), P("temp", "dom"), P("temp"))
    return jax.shard_map(
        per_device, mesh=mesh, in_specs=in_specs, out_specs=out_specs, check_vma=False
    )
```

profile of v0, /device:TPU:0, one launch (start us, length us, event | category | flops | bytes accessed | tf_op | source)
XLA Modules:
  0.0 235.8 jit_solution(7733646475601263255)
XLA Ops:
  7.2 0.8 compare_convert_fusion.1
  8.2 1.4 fusion.120
  11.6 1.8 dynamic-slice_select_fusion
  13.4 1.4 fusion.97
  14.8 22.2 %all-gather.1 = f32[8,1,2]{2,1,0:T(1,128)S(1)} all-gather(f32[1,1,2]{2,1,0:T(1,128)S(1)} %fusion.97), channel_id=1, replica_groups=mesh['temp'=4,'dom'=8] {'dom'}, dimensions={0}, use_global_device_ids=true | all-gather | bytes 72 | tf_op jit(solution)/shard_map/all_gather | solution.py:117
  37.5 0.7 fusion.93
  38.2 1.3 fusion.94
  40.1 0.6 fusion.95
  42.9 0.8 reduce-window.37
  43.7 0.8 reduce-window.38
  45.0 0.7 compare_bitcast_fusion.2
  46.3 0.7 compare_bitcast_fusion.3
  49.3 27.5 %all-gather.5.cloned.1.call-done = bf16[1,512,3072]{2,1,0:T(8,128)(2,1)} async-done(((bf16[1,64,3072]{2,1,0:T(8,128)(2,1)}), bf16[1,512,3072]{2,1,0:T(8,128)(2,1)}) %all-gather.5.cloned.1.call-update) | async-done | bytes 3145744 | tf_op jit(solution)/shard_map/all_gather | solution.py:139
  76.8 2.8 %convolution_convert_fusion = bf16[64,3072]{1,0:T(8,128)(2,1)S(1)} fusion(bf16[1,512,3072]{2,1,0:T(8,128)(2,1)} %all-gather.5.cloned.1.call-done, s32[64]{0:T(128)} %iota_add_fusion, pred[]{:T(512)S(6)} %lt.54), kind=kOutput, calls=%fused_computation.5 | convolution fusion | flops 201588736 | bytes 3539201 | tf_op jit(solution)/shard_map/dot_general | solution.py:144
  79.7 2.3 select_select_fusion.2
  81.9 3.4 %gather_fusion.1 = bf16[2,64,3072]{2,1,0:T(8,128)(2,1)} fusion(bf16[8,64,3072]{2,1,0:T(8,128)(2,1)} %select_select_fusion.2, s32[1024]{0:T(1024)S(1)} %pad_clamp_fusion.4), kind=kCustom, calls=%fused_computation.clone | custom fusion | bytes 1572872 | tf_op jit(solution)/shard_map/jit(_take)/gather | solution.py:72
  85.3 2.1 broadcast_select_fusion.1
  87.5 1.3 collective-permute-start
  88.7 3.9 %collective-permute-start.1 = (bf16[128,3072]{1,0:T(8,128)(2,1)}, bf16[128,3072]{1,0:T(8,128)(2,1)}, u32[]{:S(2)}, u32[]{:S(2)}) collective-permute-start(bf16[128,3072]{1,0:T(8,128)(2,1)} %bitcast.21), channel_id=1, source_target_pairs={{0,8},{8,16},{16,24},{1,9},{9,17},{17,25},{2,10},{10,18},{18,26},{... | collective-permute-start | bytes 2359304 | tf_op jit(solution)/shard_map/ppermute | solution.py:20
  93.7 0.7 reduce.24
  95.7 1.2 pad_clamp_fusion
  96.9 0.7 log_bitcast_fusion
  97.6 0.7 broadcast_subtract_fusion
  98.3 2.1 broadcast_select_fusion.2
  100.4 3.5 %gather_fusion.2 = bf16[8,64,3072]{2,1,0:T(8,128)(2,1)} fusion(bf16[2,64,3072]{2,1,0:T(8,128)(2,1)} %bitcast.77, s32[1024]{0:T(1024)S(1)} %pad_clamp_fusion.3), kind=kCustom, calls=%fused_computation.1.clone | custom fusion | bytes 6291488 | tf_op jit(solution)/shard_map/jit(_take)/gather | solution.py:79
  103.9 5.2 %select_select_fusion.1 = bf16[8,64,3072]{2,1,0:T(8,128)(2,1)} fusion(bf16[8,64,3072]{2,1,0:T(8,128)(2,1)} %gather_fusion.2, pred[8]{0:T(512)(128)(4,1)} %get-tuple-element.41, pred[8]{0:T(512)(128)(4,1)} %copy-done.13, bf16[8,64,3072]{2,1,0:T(8,128)(2,1)} %bitcast.80, bf16[64,3072]{1,0:T(8,128)(2,1)S(1)} %convolution_convert_fusion, ...), kind=kLoop, calls=%fused_computation.13 | loop fusion | flops 6291456 | bytes 9830432 | tf_op jit(solution)/shard_map/jit(_where)/select_n | solution.py:79
  109.1 3.4 %gather_fusion.3 = bf16[2,64,3072]{2,1,0:T(8,128)(2,1)} fusion(bf16[8,64,3072]{2,1,0:T(8,128)(2,1)} %select_select_fusion.1, s32[1024]{0:T(1024)S(1)} %pad_clamp_fusion.2), kind=kCustom, calls=%fused_computation.2.clone | custom fusion | bytes 1572872 | tf_op jit(solution)/shard_map/jit(_take)/gather | solution.py:72
  112.5 2.2 broadcast_select_fusion
  114.7 1.3 collective-permute-start.2
  116.0 7.3 %collective-permute-start.3 = (bf16[128,3072]{1,0:T(8,128)(2,1)}, bf16[128,3072]{1,0:T(8,128)(2,1)}, u32[]{:S(2)}, u32[]{:S(2)}) collective-permute-start(bf16[128,3072]{1,0:T(8,128)(2,1)} %bitcast.23), channel_id=1, source_target_pairs={{0,8},{8,16},{16,24},{1,9},{9,17},{17,25},{2,10},{10,18},{18,26},{... | collective-permute-start | bytes 2359304 | tf_op jit(solution)/shard_map/ppermute | solution.py:20
  123.2 0.7 fusion.91
  123.9 18.3 %all-gather.2 = f32[8,1,64]{2,1,0:T(1,128)S(1)} all-gather(f32[1,1,64]{2,1,0:T(1,128)S(1)} %fusion.91), channel_id=1, replica_groups=mesh['temp'=4,'dom'=8] {'dom'}, dimensions={0}, use_global_device_ids=true | all-gather | bytes 2304 | tf_op jit(solution)/shard_map/all_gather | solution.py:118
  142.2 0.7 reduce.25
  143.0 0.9 gather_fusion
  145.3 2.1 broadcast_select_fusion.3
  147.4 3.5 %gather_fusion.4 = bf16[8,64,3072]{2,1,0:T(8,128)(2,1)} fusion(bf16[2,64,3072]{2,1,0:T(8,128)(2,1)} %bitcast.78, s32[1024]{0:T(1024)S(1)} %pad_clamp_fusion.1), kind=kCustom, calls=%fused_computation.3.clone | custom fusion | bytes 6291488 | tf_op jit(solution)/shard_map/jit(_take)/gather | solution.py:79
  151.0 3.3 %select_select_fusion = bf16[8,64,3072]{2,1,0:T(8,128)(2,1)S(1)} fusion(bf16[8,64,3072]{2,1,0:T(8,128)(2,1)} %select_select_fusion.1, bf16[8,64,3072]{2,1,0:T(8,128)(2,1)} %gather_fusion.4, pred[8]{0:T(512)(128)(4,1)S(1)} %get-tuple-element.39, pred[8]{0:T(512)(128)(4,1)S(1)} %copy-done.12), kind=kLoop, calls=%fused_computation.12 | loop fusion | flops 3145728 | bytes 9437200 | tf_op jit(solution)/shard_map/jit(_where)/select_n | solution.py:79
  154.3 1.2 slice.53
  155.5 0.9 copy-done.2
  156.8 2.1 fusion.121
  158.9 6.4 %fusion.61 = f32[512,3072]{1,0:T(8,128)} fusion(bf16[512,3072]{1,0:T(8,128)(2,1)S(1)} %copy-done, bf16[512,512]{1,0:T(8,128)(2,1)} %param.23, f32[512,512]{1,0:T(8,128)} %fusion.121), kind=kOutput, calls=%fused_computation.80 | convolution fusion | flops 1883766784 | bytes 11010048 | tf_op jit(solution)/shard_map/dot_general | solution.py:38
  165.3 5.8 %fusion.3 = (f32[512]{0:T(512)S(1)}, bf16[512,1536]{1,0:T(8,128)(2,1)}) fusion(f32[512,3072]{1,0:T(8,128)} %fusion.61, bf16[512,3072]{1,0:T(8,128)(2,1)} %bitcast.84), kind=kLoop, calls=%fused_computation.15 | loop fusion | flops 4718080 | bytes 9439232 | tf_op jit(solution)/shard_map/reduce_sum | solution.py:43
  171.1 5.4 %fusion.56 = f32[512]{0:T(512)S(1)} fusion(bf16[512,512]{1,0:T(8,128)(2,1)} %param.26, f32[512]{0:T(512)S(1)} %copy-done.15, bf16[512,3072]{1,0:T(8,128)(2,1)} %bitcast.85, bf16[3072,512]{1,0:T(8,128)(2,1)} %param.25), kind=kOutput, calls=%fused_computation.74 | convolution fusion | flops 1884028416 | bytes 6819840 | tf_op jit(solution)/shard_map/dot_general | solution.py:50
  176.5 5.5 %fusion.39 = f32[512]{0:T(512)S(1)} fusion(bf16[512,512]{1,0:T(8,128)(2,1)} %param.26, bf16[3072,512]{1,0:T(8,128)(2,1)} %param.25, bf16[512,1536]{1,0:T(8,128)(2,1)} %get-tuple-element.44, bf16[512,1536]{1,0:T(8,128)(2,1)} %slice.53, f32[512]{0:T(512)S(1)} %copy-done.15), kind=kOutput, calls=%fused_computation.57 | convolution fusion | flops 1890319872 | bytes 6819840 | tf_op jit(solution)/shard_map/dot_general | solution.py:50
  182.0 3.9 %fusion.5 = bf16[1,512,3072]{2,1,0:T(8,128)(2,1)} fusion(bf16[512,1536]{1,0:T(8,128)(2,1)} %get-tuple-element.44, bf16[512,1536]{1,0:T(8,128)(2,1)} %slice.53), kind=kLoop, calls=%fused_computation.17 | loop fusion | flops 6291456 | bytes 6291456 | tf_op jit(solution)/shard_map/reshape | solution.py:170
  186.5 17.8 %pmax.7 = f32[]{:T(128)} all-reduce(f32[]{:T(128)} %get-tuple-element.36), channel_id=1, replica_groups=mesh['temp'=4,'dom'=8] {'dom'}, use_global_device_ids=true, to_apply=%region_19.22 | all-reduce | flops 1 | bytes 8 | tf_op jit(solution)/shard_map/pmax | solution.py:163
  204.2 1.3 exponential_reduce_fusion
  205.6 19.7 %all-reduce = (f32[]{:T(128)}, f32[]{:T(128)}) all-reduce(f32[]{:T(128)} %get-tuple-element.28, f32[]{:T(128)} %get-tuple-element.27), channel_id=1, replica_groups=mesh['temp'=4,'dom'=8] {'dom'}, use_global_device_ids=true, to_apply=%region_21.24 | all-reduce | flops 2 | bytes 16 | tf_op jit(solution)/shard_map/psum | solution.py:164
  (78 shorter events, 9.2 us)
Async XLA Ops:
  7.2 151.8 %copy-start = (bf16[512,3072]{1,0:T(8,128)(2,1)S(1)}, bf16[512,3072]{1,0:T(8,128)(2,1)}, u32[]{:S(2)}) copy-start(bf16[512,3072]{1,0:T(8,128)(2,1)} %param.24) | copy-start | bytes 9437188
  7.2 69.6 %all-gather.5.cloned.1.call-start = ((), (), s32[]{:S(2)}) async-start(), calls=%async_computation | async-start | bytes 3538944 | tf_op jit(solution)/shard_map/all_gather | solution.py:139
  8.0 73.9 %copy-start.6 = (pred[8]{0:T(512)(128)(4,1)}, pred[8]{0:T(512)(128)(4,1)S(1)}, u32[]{:S(2)}) copy-start(pred[8]{0:T(512)(128)(4,1)S(1)} %get-tuple-element.49) | copy-start | bytes 28
  44.5 4.7 %copy-start.16 = (s32[8,1]{0,1:T(1,128)}, s32[8,1]{0,1:T(1,128)S(1)}, u32[]{:S(2)}) copy-start(s32[8,1]{0,1:T(1,128)S(1)} %reduce-window.38) | copy-start | bytes 100
  45.7 0.5 copy-start.13
  47.0 0.5 copy-start.11
  48.2 31.4 %copy-start.4 = (pred[8]{0:T(512)(128)(4,1)}, pred[8]{0:T(512)(128)(4,1)S(1)}, u32[]{:S(2)}) copy-start(pred[8]{0:T(512)(128)(4,1)S(1)} %compare_bitcast_fusion) | copy-start | bytes 28
  76.8 2.9 %copy-start.1 = (bf16[1,512,3072]{2,1,0:T(8,128)(2,1)S(1)}, bf16[1,512,3072]{2,1,0:T(8,128)(2,1)}, u32[]{:S(2)}) copy-start(bf16[1,512,3072]{2,1,0:T(8,128)(2,1)} %param.16) | copy-start | bytes 9437188
  81.9 11.8 %copy-start.3 = (f32[1,512]{1,0:T(1,128)S(1)}, f32[1,512]{1,0:T(1,128)}, u32[]{:S(2)}) copy-start(f32[1,512]{1,0:T(1,128)} %param.17) | copy-start | bytes 6148
  87.5 10.8 %collective-permute-start = (bf16[128,3072]{1,0:T(8,128)(2,1)}, bf16[128,3072]{1,0:T(8,128)(2,1)}, u32[]{:S(2)}, u32[]{:S(2)}) collective-permute-start(bf16[128,3072]{1,0:T(8,128)(2,1)} %bitcast.21), channel_id=1, source_target_pairs={{8,0},{16,8},{24,16},{9,1},{17,9},{25,17},{10,2},{18,10},{26,18},{... | collective-permute-start | bytes 2359304 | tf_op jit(solution)/shard_map/ppermute | solution.py:23
  88.7 9.5 %collective-permute-start.1 = (bf16[128,3072]{1,0:T(8,128)(2,1)}, bf16[128,3072]{1,0:T(8,128)(2,1)}, u32[]{:S(2)}, u32[]{:S(2)}) collective-permute-start(bf16[128,3072]{1,0:T(8,128)(2,1)} %bitcast.21), channel_id=1, source_target_pairs={{0,8},{8,16},{16,24},{1,9},{9,17},{17,25},{2,10},{10,18},{18,26},{... | collective-permute-start | bytes 2359304 | tf_op jit(solution)/shard_map/ppermute | solution.py:20
  97.6 0.7 copy-start.9
  100.4 3.5 %copy-start.5 = (pred[8]{0:T(512)(128)(4,1)S(1)}, pred[8]{0:T(512)(128)(4,1)}, u32[]{:S(2)}) copy-start(pred[8]{0:T(512)(128)(4,1)} %copy-done.4) | copy-start | bytes 28
  103.9 8.6 %copy-start.8 = (pred[2]{0:T(512)(128)(4,1)S(1)}, pred[2]{0:T(512)(128)(4,1)}, u32[]{:S(2)}) copy-start(pred[2]{0:T(512)(128)(4,1)} %get-tuple-element.52) | copy-start | bytes 10
  109.1 35.0 %copy-start.7 = (pred[8]{0:T(512)(128)(4,1)S(1)}, pred[8]{0:T(512)(128)(4,1)}, u32[]{:S(2)}) copy-start(pred[8]{0:T(512)(128)(4,1)} %copy-done.6) | copy-start | bytes 28
  109.1 35.3 %copy-start.10 = (f32[8]{0:T(128)S(1)}, f32[8]{0:T(128)}, u32[]{:S(2)}) copy-start(f32[8]{0:T(128)} %copy-done.9) | copy-start | bytes 100
  109.1 36.1 %copy-start.17 = (s32[8,1]{0,1:T(1,128)S(1)}, s32[8,1]{0,1:T(1,128)}, u32[]{:S(2)}) copy-start(s32[8,1]{0,1:T(1,128)} %copy-done.16) | copy-start | bytes 100
  114.7 30.6 %collective-permute-start.2 = (bf16[128,3072]{1,0:T(8,128)(2,1)}, bf16[128,3072]{1,0:T(8,128)(2,1)}, u32[]{:S(2)}, u32[]{:S(2)}) collective-permute-start(bf16[128,3072]{1,0:T(8,128)(2,1)} %bitcast.23), channel_id=1, source_target_pairs={{8,0},{16,8},{24,16},{9,1},{17,9},{25,17},{10,2},{18,10},{26,18},{... | collective-permute-start | bytes 2359304 | tf_op jit(solution)/shard_map/ppermute | solution.py:23
  116.0 29.4 %collective-permute-start.3 = (bf16[128,3072]{1,0:T(8,128)(2,1)}, bf16[128,3072]{1,0:T(8,128)(2,1)}, u32[]{:S(2)}, u32[]{:S(2)}) collective-permute-start(bf16[128,3072]{1,0:T(8,128)(2,1)} %bitcast.23), channel_id=1, source_target_pairs={{0,8},{8,16},{16,24},{1,9},{9,17},{17,25},{2,10},{10,18},{18,26},{... | collective-permute-start | bytes 2359304 | tf_op jit(solution)/shard_map/ppermute | solution.py:20
  147.4 3.6 %copy-start.12 = (pred[8]{0:T(512)(128)(4,1)S(1)}, pred[8]{0:T(512)(128)(4,1)}, u32[]{:S(2)}) copy-start(pred[8]{0:T(512)(128)(4,1)} %copy-done.11) | copy-start | bytes 28
  154.3 2.2 copy-start.2
  154.3 2.6 %copy-start.14 = (bf16[1536,512]{1,0:T(8,128)(2,1)S(1)}, bf16[1536,512]{1,0:T(8,128)(2,1)}, u32[]{:S(2)}) copy-start(bf16[1536,512]{1,0:T(8,128)(2,1)} %param.22) | copy-start | bytes 4718596
  165.3 5.8 %copy-start.15 = (f32[512]{0:T(512)S(1)}, f32[512]{0:T(512)}, u32[]{:S(2)}) copy-start(f32[512]{0:T(512)} %param.27) | copy-start | bytes 6148
Sparse Core Ops, SparseCore 0:
  13.5 63.2 all-gather.4
where the time goes:
time: 237 us; the launch traced here: 236 us
  blocking collectives  78 us (33%)
  other arithmetic  52 us (22%)
  waiting for transfers between devices  27.6 us (12%)
  between operations  22.4 us (9%)
  matrix products  22.1 us (9%)
  local copies, waits for them, and re-layouts  19.9 us (8%)
  starting transfers between devices  13.8 us (6%)
    all_gather x1, waiting for transfers between devices, per_device(): shard_rows = lax.all_gather(spare_blocks, 'dom', axis=0, tiled=True)  27.5 us
    all_gather x1, blocking collectives, per_device(): lax.all_gather(own_tally, 'dom', axis=0, tiled=True)  22.2 us
    psum x1, blocking collectives, per_device(): lax.psum((jnp.sum(jnp.exp(updated - peak)), jnp.sum(jnp.exp(2.0 * (update...  19.7 us
    all_gather x1, blocking collectives, per_device(): lax.all_gather(spare_weights, 'dom', axis=0, tiled=True)  18.3 us
    pmax x1, blocking collectives, per_device(): peak = lax.pmax(jnp.max(updated), 'dom')  17.8 us
    ppermute x2, starting transfers between devices, with_halo(): lax.ppermute(lax.slice_in_dim(block, block.shape[dim] - width, None, axis...  11.2 us
    dot_general x2, matrix products, energy(): jnp.dot(layer_one, energy_mid, preferred_element_type=jnp.float32)  10.9 us
    select_n x2, other arithmetic, neighbour_swap(): jnp.where((swap_mask == 1)[:, None, None], jnp.take(received, placed_at,...  8.45 us
  transfers between devices with their start and end apart: 5, of which 1 were waited for; matrix products, arithmetic and copies ran while one was open for 8% of the time, Pallas kernels for 0%

commit v1 on v0

v1 whole, which is shorter than its diff:
```python
import functools

import jax
import jax.numpy as jnp
from jax import lax
from jax.experimental import pallas as pl
from jax.experimental.pallas import tpu as pltpu
from jax.sharding import PartitionSpec as P

SWAPS = 2
LANES = 128
TILE = 256

old_level = 0.5
new_level = 0.75
scale_limit = 0.05
MESH = pl.DeviceIdType.MESH


def gelu(x):
    return 0.5 * x * (1.0 + jnp.tanh(0.7978845608028654 * (x + 0.044715 * (x * x * x))))


def dot(a, b):
    return jnp.dot(a, b, preferred_element_type=jnp.float32)


def fold(x):
    total = x[:, :LANES]
    for c in range(LANES, x.shape[1], LANES):
        total = total + x[:, c : c + LANES]
    return total


def lane_sums(x):
    return [
        jnp.sum(jnp.transpose(x[i : i + LANES]), axis=0, keepdims=True)
        for i in range(0, x.shape[0], LANES)
    ]


def kernel(
    n,
    groups,
    nb,
    off,
    even,
    odd,
    inv,
    logw,
    eout,
    part,
    fin,
    fmid,
    fout,
    ein,
    emid,
    out,
    nlw,
    ess,
    p0,
    p1,
    n1,
    wfin,
    wfmid,
    wfout,
    wein,
    wemid,
    g0,
    g1,
    es0,
    es1,
    er0,
    er1,
    os0,
    os1,
    or0,
    or1,
    tal,
    tals,
    tg,
    qg,
    xes,
    xer,
    xos,
    xor_,
    load_sem,
    smem_sem,
    ring_send,
    ring_recv,
    all_send,
    all_recv,
    swap_send,
    swap_recv,
    tiny_send,
    tiny_recv,
):
    br = part.shape[1]
    half = part.shape[2] // 2
    rows = nb * br
    per = LANES // br
    srows = rows // LANES
    me = lax.axis_index("dom")
    grp = lax.axis_index("temp")
    has_odd = (grp > 0) & (grp < groups - 1)
    even_dev = grp + 1 - 2 * (grp % 2)
    odd_dev = grp - 1 + 2 * (grp % 2)

    loads = [
        pltpu.make_async_copy(part.at[:, :, pl.ds(0, half)], p0.at[pl.ds(0, nb)], load_sem.at[0]),
        pltpu.make_async_copy(fin, wfin, load_sem.at[1]),
        pltpu.make_async_copy(fmid, wfmid, load_sem.at[2]),
        pltpu.make_async_copy(fout, wfout, load_sem.at[3]),
        pltpu.make_async_copy(part.at[:, :, pl.ds(half, half)], p1, load_sem.at[4]),
        pltpu.make_async_copy(ein, wein, load_sem.at[5]),
        pltpu.make_async_copy(emid, wemid, load_sem.at[6]),
    ]
    for c in loads:
        c.start()

    for ref in (or0, or1, xor_):
        ref[...] = jnp.zeros(ref.shape, ref.dtype)

    barrier = pltpu.get_barrier_semaphore()
    for k in range(1, n):
        pl.semaphore_signal(
            barrier, inc=1, device_id={"dom": lax.rem(me + k, n)}, device_id_type=MESH
        )
    pl.semaphore_signal(barrier, inc=1, device_id={"temp": even_dev}, device_id_type=MESH)

    @pl.when(has_odd)
    def _():
        pl.semaphore_signal(barrier, inc=1, device_id={"temp": odd_dev}, device_id_type=MESH)

    spare = jnp.int32(0)
    vacant = jnp.int32(-1)
    dd = jnp.int32(0)
    vv = jnp.int32(0)
    cnt = [off[0, j] for j in range(nb)]
    ev = [even[0, j] for j in range(nb)]
    od = [odd[0, j] for j in range(nb)]
    for j in range(nb):
        spare = jnp.where(cnt[j] == 2, j, spare)
        vacant = jnp.where(cnt[j] == 0, j, vacant)
        dd = jnp.where(cnt[j] == 2, 1, dd)
        vv = jnp.where(cnt[j] == 0, 1, vv)

    def ranks(flags):
        seen = jnp.int32(0)
        rank = []
        chosen = [jnp.int32(0)] * SWAPS
        for j in range(nb):
            rank.append(jnp.minimum(seen, SWAPS - 1))
            for s in range(SWAPS):
                chosen[s] = jnp.where((flags[j] == 1) & (seen == s), j, chosen[s])
            seen = seen + flags[j]
        return rank, chosen

    erank, echosen = ranks(ev)
    orank, ochosen = ranks(od)

    def pick(values, index):
        total = values[0]
        for j in range(1, len(values)):
            total = jnp.where(index == j, values[j], total)
        return total

    loads[0].wait()
    g0[me] = p0[spare]
    tal[me] = jnp.full((8, LANES), dd + 2 * vv, jnp.int32)

    @pl.when(has_odd)
    def _():
        pl.semaphore_wait(barrier, n + 1)

    @pl.when(jnp.logical_not(has_odd))
    def _():
        pl.semaphore_wait(barrier, n)

    odd_me = me % 2
    pos = (1 - odd_me) * (me // 2) + odd_me * (n - 1 - me // 2)

    def dom_of(p):
        p = (p + 2 * n) % n
        hi = p // (n // 2)
        return (1 - hi) * (2 * p) + hi * (2 * (n - 1 - p) + 1)

    g = (g0, g1)
    steps = n - 1
    cr = br // 2

    def ring_copy(h, way, s, receiving):
        d = s // 2 + 1
        r = (s % 2 + way) % 2
        sign = 1 - 2 * way
        owner = dom_of(pos - sign * (d if receiving else d - 1))
        view = g[h].at[owner, pl.ds(r * cr, cr)]
        return pltpu.make_async_remote_copy(
            src_ref=view,
            dst_ref=view,
            send_sem=ring_send.at[h, way, s],
            recv_sem=ring_recv.at[h, way, s],
            device_id={"dom": dom_of(pos + sign)},
            device_id_type=MESH,
        )

    def ring_step(h, s):
        for way in range(2):
            if s >= 2:
                ring_copy(h, way, s - 2, True).wait_recv()
            ring_copy(h, way, s, False).start()

    def ring_end(h):
        for s in range(max(steps - 2, 0), steps):
            for way in range(2):
                ring_copy(h, way, s, True).wait_recv()

    pending = [(0, s) for s in range(steps)]

    def pump(count):
        for _ in range(min(count, len(pending))):
            ring_step(*pending.pop(0))

    def share(index, ref, receiving, k):
        view = ref.at[lax.rem(me - k + n, n)] if receiving else ref.at[me]
        return pltpu.make_async_remote_copy(
            src_ref=view,
            dst_ref=view,
            send_sem=all_send.at[index, k],
            recv_sem=all_recv.at[index, k],
            device_id={"dom": lax.rem(me + k, n)},
            device_id_type=MESH,
        )

    def share_start(index, ref):
        for k in range(1, n):
            share(index, ref, False, k).start()

    def share_wait(index, ref):
        for k in range(1, n):
            share(index, ref, True, k).wait_recv()

    pump(2)
    share_start(0, tal)

    tiles = rows // TILE
    lds = []
    wide = 512
    for c in loads[1:5]:
        c.wait()
    tb = TILE // br

    def tall(ref, t, cols=slice(None)):
        x = ref[t * tb : (t + 1) * tb, :, cols]
        return x.reshape(TILE, x.shape[2])

    for t in range(tiles):
        rs = slice(t * tb, (t + 1) * tb)
        hid = gelu(dot(tall(p0, t), wfin[...])).astype(jnp.bfloat16)
        hid = gelu(dot(hid, wfmid[...])).astype(jnp.bfloat16)
        total = jnp.zeros((TILE, LANES), jnp.float32)
        for c in range(0, half, wide):
            ls = scale_limit * jnp.tanh(dot(hid, wfout[:, c : c + wide]))
            shift = dot(hid, wfout[:, half + c : half + c + wide])
            new = tall(p1, t, slice(c, c + wide)).astype(jnp.float32) * jnp.exp(ls) + shift
            n1[rs, :, c : c + wide] = new.astype(jnp.bfloat16).reshape(tb, br, wide)
            total = total + fold(ls)
        lds += lane_sums(total)
        pump(1)
    g1[me] = n1[spare]
    pending += [(1, s) for s in range(steps)]

    share_wait(0, tal)
    down = pltpu.make_async_copy(tal, tals, smem_sem)
    down.start()
    down.wait()
    my_rank = jnp.int32(0)
    codes = [tals[o, 0, 0] for o in range(n)]
    for o in range(n):
        my_rank = my_rank + jnp.where(o < me, codes[o] // 2, 0)
    source = jnp.int32(0)
    seen = jnp.int32(0)
    for o in range(n):
        has = codes[o] % 2
        source = jnp.where((has == 1) & (seen == my_rank), o, source)
        seen = seen + has

    loads[5].wait()
    loads[6].wait()
    us = []
    for t in range(tiles):
        low = dot(tall(p0, t), wein[:half, :])

        def energy(v, low):
            layer = gelu(low + dot(v, wein[half:, :])).astype(jnp.bfloat16)
            return fold(gelu(dot(layer, wemid[...])) * eout[...])

        before = energy(tall(p1, t), low)
        pump(1)
        after = energy(tall(n1, t), low)
        us += lane_sums(new_level * after - old_level * before)
        pump(1)

    lane = lax.broadcasted_iota(jnp.int32, (srows, LANES), 1)
    row = lax.broadcasted_iota(jnp.int32, (srows, LANES), 0)
    slot = row * per + lane // br

    def spread(values):
        total = jnp.zeros((srows, LANES), jnp.int32)
        for j in range(nb):
            total = jnp.where(slot == j, values[j], total)
        return total

    counts = spread(cnt)
    kept = logw[...] - jnp.log(jnp.maximum(counts, 1).astype(jnp.float32))
    mine = tg.at[me]
    tg[me] = jnp.zeros((tg.shape[1], LANES), jnp.float32)
    for i in range(srows):
        mine[i : i + 1, :] = lds[i]
        mine[srows + i : srows + i + 1, :] = us[i]
    own_ld = mine[0:srows, :]
    own_u = mine[srows : 2 * srows, :]
    lane1 = lax.broadcasted_iota(jnp.int32, (1, LANES), 1)
    for i, values in enumerate((own_ld, own_u, kept)):
        v = pick([values[j : j + 1, :] for j in range(srows)], spare // per)
        turned = pltpu.roll(v, br, 1)
        mine[2 * srows + i : 2 * srows + i + 1, :] = jnp.where(
            lane1 // br == spare % per, v, turned
        )
    share_start(1, tg)
    pump(1)
    share_wait(1, tg)
    fill = tg[source]
    vmask = slot == vacant

    def filled(i, values):
        return jnp.where(
            vmask, jnp.broadcast_to(fill[2 * srows + i : 2 * srows + i + 1, :], values.shape), values
        )

    ld = filled(0, own_ld)
    u = filled(1, own_u)
    weight = filled(2, kept)

    def swap_copy(index, sems, src, dst, device):
        return pltpu.make_async_remote_copy(
            src_ref=src,
            dst_ref=dst,
            send_sem=sems[0].at[index],
            recv_sem=sems[1].at[index],
            device_id={"temp": device},
            device_id_type=MESH,
        )

    tiny = (tiny_send, tiny_recv)
    big = (swap_send, swap_recv)
    xes[0:srows, :] = ld
    xes[srows : 2 * srows, :] = u
    tiny_even = swap_copy(0, tiny, xes, xer, even_dev)
    tiny_even.start()
    emask = spread(ev) == 1
    omask = spread(od) == 1
    pump(1)
    tiny_even.wait()
    ld = jnp.where(emask, xer[0:srows, :], ld)
    u = jnp.where(emask, xer[srows : 2 * srows, :], u)
    xos[0:srows, :] = ld
    xos[srows : 2 * srows, :] = u
    tiny_odd = swap_copy(1, tiny, xos, xor_, odd_dev)

    stock = (p0, n1)
    sends_e, gets_e = (es0, es1), (er0, er1)
    sends_o, gets_o = (os0, os1), (or0, or1)
    resampled = [jnp.where(cnt[j] == 0, nb, j) for j in range(nb)]
    evened = [jnp.where(ev[j] == 1, nb + 1 + erank[j], resampled[j]) for j in range(nb)]
    final = [jnp.where(od[j] == 1, nb + 1 + SWAPS + orank[j], evened[j]) for j in range(nb)]

    def even_copy(h):
        return swap_copy(h, big, sends_e[h], gets_e[h], even_dev)

    def odd_copy(h):
        return swap_copy(2 + h, big, sends_o[h], gets_o[h], odd_dev)

    def even_send(h):
        stock[h][nb] = g[h][source]
        for s in range(SWAPS):
            sends_e[h][s] = stock[h][pick(resampled, echosen[s])]
        even_copy(h).start()

    def odd_send(h):
        even_copy(h).wait()
        stock[h][nb + 1 : nb + 1 + SWAPS] = gets_e[h][...]
        for s in range(SWAPS):
            sends_o[h][s] = stock[h][pick(evened, ochosen[s])]

        @pl.when(has_odd)
        def _():
            odd_copy(h).start()

    def finish(h):
        @pl.when(has_odd)
        def _():
            odd_copy(h).wait()

        stock[h][nb + 1 + SWAPS :] = gets_o[h][...]
        for j in range(nb):
            out[j, :, h * half : (h + 1) * half] = stock[h][final[j]]

    ring_end(0)
    even_send(0)

    @pl.when(has_odd)
    def _():
        tiny_odd.start()

    pump(1)
    odd_send(0)
    pump(1)

    @pl.when(has_odd)
    def _():
        tiny_odd.wait()

    ld = jnp.where(omask, xor_[0:srows, :], ld)
    u = jnp.where(omask, xor_[srows : 2 * srows, :], u)
    updated = weight + ld - inv[0] * u

    def everywhere(x):
        return jnp.broadcast_to(x, (1, LANES))

    def whole(reduce, x):
        return everywhere(reduce(reduce(x, axis=0, keepdims=True), axis=1, keepdims=True))

    own_peak = whole(jnp.max, updated)
    qmine = qg.at[me]
    qg[me] = jnp.zeros((qg.shape[1], LANES), jnp.float32)
    qmine[0:1, :] = own_peak
    qmine[1:2, :] = whole(jnp.sum, jnp.exp(updated - own_peak))
    qmine[2:3, :] = whole(jnp.sum, jnp.exp(2.0 * (updated - own_peak)))
    share_start(2, qg)
    pump(1)
    finish(0)
    pump(1)
    share_wait(2, qg)
    pump(len(pending))
    peak = qg[0, 0:1, :]
    for o in range(1, n):
        peak = jnp.maximum(peak, qg[o, 0:1, :])
    first = jnp.zeros((1, LANES), jnp.float32)
    second = jnp.zeros((1, LANES), jnp.float32)
    for o in range(n):
        lower = qg[o, 0:1, :] - peak
        first = first + qg[o, 1:2, :] * jnp.exp(lower)
        second = second + qg[o, 2:3, :] * jnp.exp(2.0 * lower)
    nlw[...] = updated - (peak + jnp.log(first))
    total = jnp.full((1, LANES), float(rows * n), jnp.float32)
    ess[...] = 2.0 * jnp.log(first) - jnp.log(second) - jnp.log(total)

    ring_end(1)
    even_send(1)
    odd_send(1)
    finish(1)

    for h in range(2):
        for s in range(steps):
            for way in range(2):
                ring_copy(h, way, s, False).wait_send()
    for index, ref in enumerate((tal, tg, qg)):
        for k in range(1, n):
            share(index, ref, False, k).wait_send()


def per_device(
    particles,
    log_weights,
    offspring,
    even_pairs,
    odd_pairs,
    inverse_temp,
    flow_in,
    flow_mid,
    flow_out,
    energy_in,
    energy_mid,
    energy_out,
):
    n = lax.axis_size("dom")
    groups = lax.axis_size("temp")
    nb = offspring.shape[1]
    rows, features = particles.shape[1:]
    half = features // 2
    br = rows // nb
    srows = rows // LANES
    hid = flow_mid.shape[0]
    bf16, f32, i32 = jnp.bfloat16, jnp.float32, jnp.int32
    smem = pl.BlockSpec(memory_space=pltpu.SMEM)
    vmem = pl.BlockSpec(memory_space=pltpu.VMEM)
    anywhere = pl.BlockSpec(memory_space=pl.ANY)
    tile_rows = -(-(2 * srows + 3) // 8) * 8
    pair_rows = -(-(2 * srows) // 8) * 8
    swap = pltpu.VMEM((SWAPS, br, half), bf16)
    dma = pltpu.SemaphoreType.DMA
    moved, weights, ess = pl.pallas_call(
        functools.partial(kernel, n, groups, nb),
        out_shape=(
            jax.ShapeDtypeStruct((nb, br, features), bf16),
            jax.ShapeDtypeStruct((srows, LANES), f32),
            jax.ShapeDtypeStruct((1, LANES), f32),
        ),
        in_specs=[smem] * 4 + [vmem] * 2 + [anywhere] * 6,
        out_specs=(vmem, vmem, vmem),
        scratch_shapes=[
            pltpu.VMEM((nb + 1 + 2 * SWAPS, br, half), bf16),
            pltpu.VMEM((nb, br, half), bf16),
            pltpu.VMEM((nb + 1 + 2 * SWAPS, br, half), bf16),
            pltpu.VMEM(flow_in.shape, bf16),
            pltpu.VMEM(flow_mid.shape, bf16),
            pltpu.VMEM(flow_out.shape, bf16),
            pltpu.VMEM(energy_in.shape, bf16),
            pltpu.VMEM(energy_mid.shape, bf16),
            pltpu.VMEM((n, br, half), bf16),
            pltpu.VMEM((n, br, half), bf16),
        ]
        + [swap] * 8
        + [
            pltpu.VMEM((n, 8, LANES), i32),
            pltpu.SMEM((n, 8, LANES), i32),
            pltpu.VMEM((n, tile_rows, LANES), f32),
            pltpu.VMEM((n, 8, LANES), f32),
        ]
        + [pltpu.VMEM((pair_rows, LANES), f32)] * 4
        + [
            dma((7,)),
            dma,
            dma((2, 2, n - 1)),
            dma((2, 2, n - 1)),
            dma((3, n)),
            dma((3, n)),
            dma((4,)),
            dma((4,)),
            dma((2,)),
            dma((2,)),
        ],
        compiler_params=pltpu.CompilerParams(
            collective_id=0, has_side_effects=True, vmem_limit_bytes=56 * 1024 * 1024
        ),
    )(
        offspring,
        even_pairs,
        odd_pairs,
        inverse_temp,
        log_weights.reshape(srows, LANES),
        energy_out.reshape(1, hid),
        particles.reshape(nb, br, features),
        flow_in,
        flow_mid,
        flow_out,
        energy_in,
        energy_mid,
    )
    return (
        moved.reshape(1, rows, features),
        weights.reshape(1, rows),
        ess[0, :1],
    )


def solution(mesh):
    in_specs = (
        P("temp", "dom", None),
        P("temp", "dom"),
        P("temp", "dom"),
        P("temp", "dom"),
        P("temp", "dom"),
        P("temp"),
        P(),
        P(),
        P(),
        P(),
        P(),
        P(),
    )
    out_specs = (P("temp", "dom", None), P("temp", "dom"), P("temp"))
    return jax.shard_map(
        per_device, mesh=mesh, in_specs=in_specs, out_specs=out_specs, check_vma=False
    )
```

time: 237 us -> 60.8 us (0.26)
  the two profiles are of different devices: /device:TPU:0 before, /device:TPU:1 now
where the time goes in v1:
time: 60.8 us; the launch traced here: 60.6 us
  Pallas kernels  53.8 us (88%)
  local copies, waits for them, and re-layouts  4.34 us (7%)
  between operations  2.47 us (4%)
    pallas_call x1, Pallas kernels, per_device(): pl.pallas_call(functools.partial(kernel, n, groups, nb), out_shape=(jax.S...  53.8 us
    unnamed x6, local copies, waits for them, and re-layouts  4.34 us

profile of v1, /device:TPU:1, one launch (start us, length us, event | category | flops | bytes accessed | tf_op | source)
XLA Modules:
  0.0 60.6 jit_solution(7145887500113245698)
XLA Ops:
  1.3 53.8 %shard_map.139 = (bf16[8,64,3072]{2,1,0:T(8,128)(2,1)}, f32[4,128]{1,0:T(4,128)}, f32[1,128]{1,0:T(1,128)}) custom-call(s32[1,8]{1,0:T(1,128)} %off.1, s32[1,8]{1,0:T(1,128)} %even.1, s32[1,8]{1,0:T(1,128)} %odd.1, f32[1]{0:T(128)S(6)} %copy.18.inv, f32[4,128]{1,0:T(4,128)} %bitcast.9, f32[1,512]{1,0:T(1,128)} %bitcast.10, bf16[8,64,3072]{2,1,0:T(8,128)(2,1)} %bitcast.8, ...), custom_call_target="tpu_custom_call" | custom-call | tf_op jit(solution)/shard_map/pallas_call | solution.py:503
  55.0 0.0 copy-start
  55.0 0.0 copy-start.1
  55.1 3.8 %copy.19 = bf16[1,512,3072]{2,1,0:T(8,128)(2,1)} copy(bf16[1,512,3072]{2,1,0:T(8,128)(2,1)} %bitcast.7) | data formatting | bytes 6291456
  58.8 0.0 copy-done
  58.8 0.6 copy.20
  59.4 0.0 copy-done.1
Async XLA Ops:
  55.0 3.8 %copy-start = (f32[4,128]{1,0:T(4,128)S(1)}, f32[4,128]{1,0:T(4,128)}, u32[]{:S(2)}) copy-start(f32[4,128]{1,0:T(4,128)} %get-tuple-element.7) | copy-start | bytes 6148
  55.0 4.4 %copy-start.1 = (f32[1,128]{1,0:T(1,128)S(1)}, f32[1,128]{1,0:T(1,128)}, u32[]{:S(2)}) copy-start(f32[1,128]{1,0:T(1,128)} %get-tuple-element.8) | copy-start | bytes 1540

commit v2 on v1

--- a/solution.py
+++ b/solution.py
@@ -258,6 +258,7 @@
         rs = slice(t * tb, (t + 1) * tb)
         hid = gelu(dot(tall(p0, t), wfin[...])).astype(jnp.bfloat16)
         hid = gelu(dot(hid, wfmid[...])).astype(jnp.bfloat16)
+        pump(1)
         total = jnp.zeros((TILE, LANES), jnp.float32)
         for c in range(0, half, wide):
             ls = scale_limit * jnp.tanh(dot(hid, wfout[:, c : c + wide]))

time: 60.8 us -> 62.1 us (1.021)
  Pallas kernels: 53.8 us -> 55.1 us
    pallas_call x1, Pallas kernels: 53.8 us -> 55.1 us  [per_device(): pl.pallas_call(functools.partial(kernel, n, groups, nb), out_shape=(jax.S...]
where the time goes in v2:
time: 62.1 us; the launch traced here: 61.9 us
  Pallas kernels  55.1 us (89%)
  local copies, waits for them, and re-layouts  4.34 us (7%)
  between operations  2.47 us (4%)
    pallas_call x1, Pallas kernels, per_device(): pl.pallas_call(functools.partial(kernel, n, groups, nb), out_shape=(jax.S...  55.1 us
    unnamed x6, local copies, waits for them, and re-layouts  4.34 us

profile of v2, /device:TPU:1, one launch (start us, length us, event | category | flops | bytes accessed | tf_op | source)
XLA Modules:
  0.0 61.9 jit_solution(8095945889744004421)
XLA Ops:
  1.3 55.1 %shard_map.139 = (bf16[8,64,3072]{2,1,0:T(8,128)(2,1)}, f32[4,128]{1,0:T(4,128)}, f32[1,128]{1,0:T(1,128)}) custom-call(s32[1,8]{1,0:T(1,128)} %off.1, s32[1,8]{1,0:T(1,128)} %even.1, s32[1,8]{1,0:T(1,128)} %odd.1, f32[1]{0:T(128)S(6)} %copy.18.inv, f32[4,128]{1,0:T(4,128)} %bitcast.9, f32[1,512]{1,0:T(1,128)} %bitcast.10, bf16[8,64,3072]{2,1,0:T(8,128)(2,1)} %bitcast.8, ...), custom_call_target="tpu_custom_call" | custom-call | tf_op jit(solution)/shard_map/pallas_call | solution.py:504
  56.4 0.0 copy-start
  56.4 0.0 copy-start.1
  56.4 3.8 %copy.19 = bf16[1,512,3072]{2,1,0:T(8,128)(2,1)} copy(bf16[1,512,3072]{2,1,0:T(8,128)(2,1)} %bitcast.7) | data formatting | bytes 6291456
  60.1 0.0 copy-done
  60.1 0.6 copy.20
  60.7 0.0 copy-done.1
Async XLA Ops:
  56.4 3.8 %copy-start = (f32[4,128]{1,0:T(4,128)S(1)}, f32[4,128]{1,0:T(4,128)}, u32[]{:S(2)}) copy-start(f32[4,128]{1,0:T(4,128)} %get-tuple-element.7) | copy-start | bytes 6148
  56.4 4.4 %copy-start.1 = (f32[1,128]{1,0:T(1,128)S(1)}, f32[1,128]{1,0:T(1,128)}, u32[]{:S(2)}) copy-start(f32[1,128]{1,0:T(1,128)} %get-tuple-element.8) | copy-start | bytes 1540
